TPU v7x, 32 devices: a whole 2x2x4 slice. The times are simulated.
32 devices in a mesh: sp: 32 (over z, y, x, core), ch: 1.
Axes of the slice: x: 2, y: 2, z: 4, core: 2. Of those that a mesh axis runs over, the one named last changes fastest.
Arguments:
- x_in: bfloat16 [256, 64, 128], P('ch', 'sp'), may hold values from -6 to 6
- gate_in: bfloat16 [256, 64, 128], P('ch', 'sp'), may hold values from -6 to 6
- conv_weight: float32 [256, 9], P('ch'), may hold values from -2 to 2
- conv_bias: float32 [256], P('ch'), may hold values from -0.5 to 0.5
- proj_weight: bfloat16 [4, 40, 256], P(None, None, 'ch'), may hold values from -0.375 to 0.375
- dt_weight: float32 [4, 256, 8], P(None, 'ch'), may hold values from -2 to 2
- dt_bias: float32 [4, 256], P(None, 'ch'), may hold values from -2 to 1
- decay_rate: float32 [4, 256, 16], P(None, 'ch'), may hold values from 0.0005 to 0.1
- skip_gain: float32 [4, 256], P(None, 'ch'), may hold values from 0.5 to 1.5
- norm_gain: float32 [256], P('ch'), may hold values from 0.5 to 1.5
- norm_bias: float32 [256], P('ch'), may hold values from -0.5 to 0.5
Outputs:
- mixed: bfloat16 [256, 64, 128], P('ch', 'sp')
All inputs are finite; a program needn't handle non-finite values.
Results may differ from a plain program's by a relative error of at most 0.014.
Values may be sent and summed in bfloat16 or wider, within the bound.
A program may use at most 64 MiB of HBM per device.

v0:
```python
import functools

import jax
import jax.numpy as jnp
from jax import lax
from jax.experimental import pallas as pl
from jax.experimental.pallas import tpu as pltpu
from jax.sharding import PartitionSpec as P

SPAN = 64
MESH = pl.DeviceIdType.MESH
LOG2E = 1.4426950408889634
BEFORE = 64


def with_halo(value, sides, width):
    for axis, dim in sides:
        peers, length = (lax.axis_size(axis), value.shape[dim])
        up = [(i, (i + 1) % peers) for i in range(peers - 1)]
        down = [(j, i) for i, j in up]
        last = lax.slice_in_dim(value, length - width, length, axis=dim)
        first = lax.slice_in_dim(value, 0, width, axis=dim)
        before = lax.ppermute(last, axis, up)
        after = lax.ppermute(first, axis, down)
        value = jnp.concatenate([before, value, after], axis=dim)
    return value


def conv_silu(padded, conv_weight, conv_bias, rows, cols):
    total = jnp.zeros((padded.shape[0], rows, cols), jnp.float32) + conv_bias[:, None, None]
    for offset in range(9):
        down_shift = offset // 3
        side_shift = offset % 3
        window = padded[:, down_shift : down_shift + rows, side_shift : side_shift + cols].astype(
            jnp.float32
        )
        total = total + conv_weight[:, offset][:, None, None] * window
    return jax.nn.silu(total).astype(jnp.bfloat16)


def steps_first(low_rank, dt_weight, dt_bias):
    length, rank, lines = low_rank.shape
    total = jnp.zeros((length, dt_weight.shape[0], lines), jnp.float32) + dt_bias[None, :, None]
    for rank_index in range(rank):
        total = (
            total
            + dt_weight[:, rank_index][None, :, None]
            * low_rank[:, rank_index].astype(jnp.float32)[:, None, :]
        )
    return jax.nn.softplus(total)


def block_scan(values, low_rank, b_coef, c_coef, dt_weight, dt_bias, rates, skip_gain, reverse):
    length, chans, lines = values.shape
    states = rates.shape[1]
    block_len = min(SPAN, length)
    count = length // block_len
    deltas = steps_first(low_rank, dt_weight, dt_bias)
    rates_turned = rates.T[:, :, None]
    skip_column = skip_gain[:, None]

    def single(state, items):
        value_now, delta_now, b_now, c_now = items
        values_now = value_now.astype(jnp.float32)
        decays = jnp.exp(-delta_now[None] * rates_turned)
        state = (
            decays * state + (delta_now * values_now)[None] * b_now.astype(jnp.float32)[:, None, :]
        )
        output = (
            jnp.sum(c_now.astype(jnp.float32)[:, None, :] * state, axis=0)
            + skip_column * values_now
        )
        return (state, output)

    def advance(state, block_items):
        return lax.scan(single, state, block_items, reverse=reverse, unroll=block_len)

    items = (
        values.reshape(count, block_len, chans, lines),
        deltas.reshape(count, block_len, chans, lines),
        b_coef.reshape(count, block_len, states, lines),
        c_coef.reshape(count, block_len, states, lines),
    )
    initial = jnp.zeros((states, chans, lines), jnp.float32)
    _, outputs = lax.scan(advance, initial, items, reverse=reverse)
    return outputs.reshape(length, chans, lines)


def two_directions(values, proj_pair, dt_weight, dt_bias, decay_rate, skip_gain, first):
    rank = dt_weight.shape[2]
    states = decay_rate.shape[2]
    total = jnp.zeros(values.shape, jnp.float32)
    for offset in range(2):
        direction = first + offset
        block = proj_pair[offset]
        total = total + block_scan(
            values,
            block[:, :rank],
            block[:, rank : rank + states],
            block[:, rank + states :],
            dt_weight[direction],
            dt_bias[direction],
            decay_rate[direction],
            skip_gain[direction],
            offset == 1,
        )
    return total


def plain_device(
    x_in,
    gate_in,
    conv_weight,
    conv_bias,
    proj_weight,
    dt_weight,
    dt_bias,
    decay_rate,
    skip_gain,
    norm_gain,
    norm_bias,
):
    chans, rows, cols = x_in.shape
    rank = dt_weight.shape[2]
    states = decay_rate.shape[2]
    width_proj = rank + 2 * states
    padded = with_halo(x_in, (("sp", 1),), 1)
    padded = jnp.pad(padded, ((0, 0), (0, 0), (1, 1)))
    conv_out = conv_silu(padded, conv_weight, conv_bias, rows, cols)
    flattened = conv_out.reshape(chans, rows * cols)
    partial_sum = jnp.dot(
        proj_weight[:2].reshape(2 * width_proj, chans),
        flattened,
        preferred_element_type=jnp.float32,
    )
    row_proj = lax.psum(partial_sum.astype(jnp.bfloat16), "ch").reshape(2, width_proj, rows, cols)
    col_in = lax.all_to_all(conv_out, "sp", split_axis=2, concat_axis=1, tiled=True)
    col_flat = col_in.reshape(chans, col_in.shape[1] * col_in.shape[2])
    col_partial = jnp.dot(
        proj_weight[2:].reshape(2 * width_proj, chans), col_flat, preferred_element_type=jnp.float32
    )
    col_proj = lax.psum(col_partial.astype(jnp.bfloat16), "ch").reshape(
        2, width_proj, col_in.shape[1], col_in.shape[2]
    )
    row_values = conv_out.transpose(2, 0, 1)
    row_pair = row_proj.transpose(0, 3, 1, 2)
    horizontal = two_directions(
        row_values, row_pair, dt_weight, dt_bias, decay_rate, skip_gain, 0
    ).transpose(1, 2, 0)
    col_values = col_in.transpose(1, 0, 2)
    col_pair = col_proj.transpose(0, 2, 1, 3)
    vertical = two_directions(col_values, col_pair, dt_weight, dt_bias, decay_rate, skip_gain, 2)
    vertical = vertical.transpose(1, 0, 2).astype(jnp.bfloat16)
    vertical_rows = lax.all_to_all(vertical, "sp", split_axis=1, concat_axis=2, tiled=True)
    combined = horizontal + vertical_rows.astype(jnp.float32)
    sum_first, sum_second = lax.psum(
        (jnp.sum(combined, axis=0), jnp.sum(combined * combined, axis=0)), "ch"
    )
    chans_total = chans * lax.axis_size("ch")
    mean = sum_first / chans_total
    var = sum_second / chans_total - mean * mean
    normed = (combined - mean[None]) * lax.rsqrt(var[None] + 1e-05) * norm_gain[
        :, None, None
    ] + norm_bias[:, None, None]
    return (normed * jax.nn.silu(gate_in.astype(jnp.float32))).astype(jnp.bfloat16)


def fused_kernel(
    n,
    x_ref,
    cw_ref,
    cb_ref,
    pw_ref,
    dw_ref,
    db_ref,
    rate_ref,
    skip_ref,
    gain_ref,
    nbias_ref,
    out_ref,
    xpad,
    halo,
    xsend,
    xrecv,
    xv,
    cr,
    wf,
    wd,
    rate_h,
    rate_v,
    u_h,
    d_h,
    p_h,
    ya_h,
    yb_h,
    state_h,
    u_v,
    d_v,
    p_v,
    ya_v,
    yb_v,
    vsend,
    vrecv,
    halo_send,
    halo_recv,
    xs_sem,
    xr_sem,
    vs_sem,
    vr_sem,
):
    rows, cols, chans = x_ref.shape
    height = rows * n
    rank = dw_ref.shape[1]
    states = rate_ref.shape[1]
    width = rank + 2 * states
    half = states // 2
    f32, bf16 = jnp.float32, jnp.bfloat16
    me = lax.axis_index("sp")
    right, left = lax.rem(me + 1, n), lax.rem(me + n - 1, n)

    barrier = pltpu.get_barrier_semaphore()

    @pl.loop(1, n)
    def _(d):
        pl.semaphore_signal(
            barrier, inc=1, device_id={"sp": lax.rem(me + d, n)}, device_id_type=MESH
        )

    edge = jnp.zeros((rows + 2, 8, chans), f32)
    xpad[:, 0:8, :] = edge
    xpad[:, cols + 8 : cols + 16, :] = edge
    for r in range(rows):
        xpad[r + 1, 8 : cols + 8, :] = x_ref[r].astype(f32)
    for j in range(n):
        at = 8 + 4 * j - 2
        pair = [xpad[r + 1, at : at + 8, :] for r in range(rows)]
        xsend[j] = jnp.concatenate(pair, axis=0).astype(bf16)
    xrecv[pl.ds(me, 1)] = xsend[pl.ds(me, 1)]

    pl.semaphore_wait(barrier, n - 1)

    def halo_copy(which):
        return pltpu.make_async_remote_copy(
            src_ref=x_ref.at[rows - 1 if which == 0 else 0],
            dst_ref=halo.at[which],
            send_sem=halo_send.at[which],
            recv_sem=halo_recv.at[which],
            device_id={"sp": right if which == 0 else left},
            device_id_type=MESH,
        )

    halo_copy(0).start()
    halo_copy(1).start()

    def x_copy(d, slot):
        dst = lax.rem(me + d, n)
        return pltpu.make_async_remote_copy(
            src_ref=xsend.at[dst],
            dst_ref=xrecv.at[slot],
            send_sem=xs_sem.at[d],
            recv_sem=xr_sem.at[d],
            device_id={"sp": dst},
            device_id_type=MESH,
        )

    def v_copy(d, slot):
        dst = lax.rem(me + d, n)
        return pltpu.make_async_remote_copy(
            src_ref=vsend.at[dst],
            dst_ref=vrecv.at[slot],
            send_sem=vs_sem.at[d],
            recv_sem=vr_sem.at[d],
            device_id={"sp": dst},
            device_id_type=MESH,
        )

    @pl.loop(1, n)
    def _(d):
        x_copy(d, me).start()

    sub = lax.broadcasted_iota(jnp.int32, (8, chans), 0)
    low4 = sub < 4
    dir_h = (sub // 2) % 2 == 0
    dir_v = low4
    low4_one = lax.broadcasted_iota(jnp.int32, (8, 128), 0) < 4

    wf[...] = jnp.zeros(wf.shape, f32)
    wd[...] = jnp.zeros(wd.shape, f32)
    for k in range(4):
        base = 128 * k
        rowsw = pw_ref[k].astype(f32)
        wf[base : base + width, :] = rowsw
        wf[base + width : base + width + rank, :] = rowsw[0:rank]
        full = dw_ref[k]
        high = full.astype(bf16).astype(f32)
        wd[base : base + rank, :] = high
        wd[base + width : base + width + rank, :] = full - high
    for s in range(states):
        rate_v[s] = -LOG2E * jnp.where(
            dir_v, rate_ref[2, s : s + 1, :], rate_ref[3, s : s + 1, :]
        )
    for s in range(half):
        lower = jnp.where(dir_h, rate_ref[0, s : s + 1, :], rate_ref[1, s : s + 1, :])
        upper = jnp.where(
            dir_h, rate_ref[0, s + half : s + half + 1, :], rate_ref[1, s + half : s + half + 1, :]
        )
        rate_h[s] = -LOG2E * jnp.where(low4, lower, upper)

    def prepare(steps, first, dirs, u, dl, p, halves):
        weights = wf[256 * first : 256 * first + 256, :].astype(bf16)
        up = wd[256 * first : 256 * first + 256, :].astype(bf16)
        bias = jnp.where(dirs, db_ref[2 * first : 2 * first + 1], db_ref[2 * first + 1 : 2 * first + 2])
        bias = bias[None]
        pick = dirs[:, 0:128][None]
        lift = low4_one[None]
        size = 16

        @pl.loop(0, steps // size)
        def _(i):
            at = pl.ds(i * size, size)
            flat = u[at].reshape(size * 8, chans).astype(bf16)
            proj = lax.dot_general(
                flat, weights, (((1,), (1,)), ((), ())), preferred_element_type=f32
            )
            proj = proj.astype(bf16).astype(f32).reshape(size, 8, 256)
            one, two = proj[:, :, 0:128], proj[:, :, 128:256]
            own = jnp.where(pick, one, two)
            both = jnp.concatenate(
                [jnp.where(pick, one, 0.0), jnp.where(pick, 0.0, two)], axis=2
            )
            pre = jnp.dot(
                both.reshape(size * 8, 256).astype(bf16), up, preferred_element_type=f32
            ).reshape(size, 8, chans)
            pre = pre + bias
            dl[at] = jnp.maximum(pre, 0.0) + jnp.log1p(jnp.exp(-jnp.abs(pre)))
            if halves:
                own = jnp.where(lift, own, pltpu.roll(own, 128 - half, 2))
            p[at] = own

    def step(t, state, u, dl, p, rate, ya, yb, last, count, offset):
        delta, tile = dl[t], p[t]
        drive = delta * u[t]
        total = None
        new = []
        for s in range(count):
            decay = jnp.exp2(delta * rate[s])
            b_now = jnp.broadcast_to(tile[:, rank + s : rank + s + 1], (8, chans))
            c_now = jnp.broadcast_to(tile[:, offset + s : offset + s + 1], (8, chans))
            now = decay * state[s] + drive * b_now
            new.append(now)
            term = c_now * now
            total = term if total is None else total + term
        for k in range(chans // 128):
            piece = total[:, k * 128 : k * 128 + 128]
            ya[k, pl.ds(pl.multiple_of(t * 8, 8), 8), :] = piece
            yb[k, pl.ds(pl.multiple_of((last - t) * 8, 8), 8), :] = piece
        return tuple(new)

    for which in range(2):
        halo_copy(which).wait()
    above, below = halo[0].astype(f32), halo[1].astype(f32)
    xpad[0, 8 : cols + 8, :] = jnp.where(me == 0, jnp.zeros_like(above), above)
    xpad[rows + 1, 8 : cols + 8, :] = jnp.where(me == n - 1, jnp.zeros_like(below), below)
    block = 32
    for r in range(rows):
        for c in range(0, cols, block):
            total = jnp.zeros((block, chans), f32) + cb_ref[...]
            for i in range(3):
                for j in range(3):
                    window = xpad[r + i, 7 + c + j : 7 + c + j + block, :]
                    total = total + cw_ref[3 * i + j : 3 * i + j + 1, :] * window
            cr[r, c : c + block, :] = jax.nn.silu(total).astype(bf16).astype(f32)

    odd = sub % 2 == 1

    def spread(t):
        ahead = jnp.where(odd, cr[1, pl.ds(t, 1), :], cr[0, pl.ds(t, 1), :])
        back = jnp.where(odd, cr[1, pl.ds(cols - 1 - t, 1), :], cr[0, pl.ds(cols - 1 - t, 1), :])
        u_h[t] = jnp.where(dir_h, ahead, back)

    @pl.loop(0, cols // 8)
    def _(i):
        for k in range(8):
            spread(i * 8 + k)

    prepare(cols, 0, dir_h, u_h, d_h, p_h, True)

    def row_steps(lower, upper, state):
        def body(t, state):
            return step(
                t, state, u_h, d_h, p_h, rate_h, ya_h, yb_h, cols - 1, half, rank + states
            )

        return lax.fori_loop(lower, upper, body, state, unroll=2)

    state = row_steps(0, BEFORE, tuple(jnp.zeros((8, chans), f32) for _ in range(half)))
    for s in range(half):
        state_h[s] = state[s]

    @pl.loop(1, n)
    def _(d):
        x_copy(d, lax.rem(me + n - d, n)).wait()

    nothing = jnp.zeros((8, chans), f32)
    xv[0] = nothing
    xv[height + 1] = nothing

    @pl.loop(0, n)
    def _(j):
        both = xrecv[j].astype(f32)
        xv[1 + 2 * j] = both[0:8]
        xv[2 + 2 * j] = both[8:16]

    def conv_step(t):
        total = jnp.zeros((8, chans), f32) + cb_ref[...]
        tiles = [xv[t], xv[t + 1], xv[t + 2]]
        for j in range(3):
            part = None
            for i in range(3):
                term = cw_ref[3 * i + j : 3 * i + j + 1, :] * tiles[i]
                part = term if part is None else part + term
            total = total + pltpu.roll(part, 7 - j, 0)
        value = jax.nn.silu(total).astype(bf16).astype(f32)
        turned = pltpu.roll(value, 4, 0)
        u_v[t, 0:4, :] = value[0:4]
        u_v[height - 1 - t, 4:8, :] = turned[4:8]

    @pl.loop(0, height // 4)
    def _(i):
        for k in range(4):
            conv_step(i * 4 + k)

    prepare(height, 1, dir_v, u_v, d_v, p_v, False)

    def col_body(t, state):
        return step(
            t, state, u_v, d_v, p_v, rate_v, ya_v, yb_v, height - 1, states, rank + states
        )

    lax.fori_loop(
        0, height, col_body, tuple(jnp.zeros((8, chans), f32) for _ in range(states)), unroll=2
    )

    skip_v = skip_ref[2:3, :] + skip_ref[3:4, :]

    def column_row(t):
        at = pl.ds(pl.multiple_of(t * 8, 8), 8)
        parts = [
            ya_v[k, at, :] + pltpu.roll(yb_v[k, at, :], 4, 0) for k in range(chans // 128)
        ]
        return jnp.concatenate(parts, axis=1) + skip_v * u_v[t]

    def column_tile(j):
        tile = jnp.where(low4, column_row(2 * j), pltpu.roll(column_row(2 * j + 1), 4, 0))
        return jnp.concatenate([tile[:, 0:128], tile[:, 128:256]], axis=0).astype(bf16)

    @pl.loop(1, n)
    def _(d):
        j = lax.rem(me + d, n)
        vsend[j] = column_tile(j)
        v_copy(d, me).start()

    vrecv[me] = column_tile(me)

    row_steps(BEFORE, cols, tuple(state_h[s] for s in range(half)))

    @pl.loop(1, n)
    def _(d):
        v_copy(d, lax.rem(me + n - d, n)).wait()

    skip_h = skip_ref[0:1, :] + skip_ref[1:2, :]

    def finish(p):
        even, other = vrecv[2 * p].astype(f32), vrecv[2 * p + 1].astype(f32)
        even = jnp.concatenate([even[0:8], even[8:16]], axis=1)
        other = jnp.concatenate([other[0:8], other[8:16]], axis=1)
        at = pl.ds(pl.multiple_of(p * 8, 8), 8)
        for r in range(rows):
            if r == 0:
                upright = jnp.where(low4, even, pltpu.roll(other, 4, 0))
            else:
                upright = jnp.where(low4, pltpu.roll(even, 4, 0), other)
            flat = skip_h * cr[r, at, :]
            for source, line in ((ya_h, r), (ya_h, 4 + r), (yb_h, 2 + r), (yb_h, 6 + r)):
                parts = [
                    source[k, pl.ds(p * 64 + line, 8, stride=8), :]
                    for k in range(chans // 128)
                ]
                flat = flat + jnp.concatenate(parts, axis=1)
            combined = flat + upright
            mean = jnp.sum(combined, axis=1, keepdims=True) / chans
            var = jnp.sum(combined * combined, axis=1, keepdims=True) / chans - mean * mean
            normed = (combined - mean) * lax.rsqrt(var + 1e-05)
            out_ref[r, at, :] = normed * gain_ref[...] + nbias_ref[...]

    @pl.loop(0, cols // 16)
    def _(i):
        finish(2 * i)
        finish(2 * i + 1)


def fused_device(
    n,
    x_in,
    gate_in,
    conv_weight,
    conv_bias,
    proj_weight,
    dt_weight,
    dt_bias,
    decay_rate,
    skip_gain,
    norm_gain,
    norm_bias,
):
    chans, rows, cols = x_in.shape
    states = decay_rate.shape[2]
    height = rows * n
    f32, bf16 = jnp.float32, jnp.bfloat16
    scratch = [
        pltpu.VMEM((rows + 2, cols + 16, chans), f32),
        pltpu.VMEM((2, cols, chans), bf16),
        pltpu.VMEM((n, 16, chans), bf16),
        pltpu.VMEM((n, 16, chans), bf16),
        pltpu.VMEM((height + 2, 8, chans), f32),
        pltpu.VMEM((rows, cols, chans), f32),
        pltpu.VMEM((512, chans), f32),
        pltpu.VMEM((512, chans), f32),
        pltpu.VMEM((states // 2, 8, chans), f32),
        pltpu.VMEM((states, 8, chans), f32),
        pltpu.VMEM((cols, 8, chans), f32),
        pltpu.VMEM((cols, 8, chans), f32),
        pltpu.VMEM((cols, 8, 128), f32),
        pltpu.VMEM((chans // 128, cols * 8, 128), f32),
        pltpu.VMEM((chans // 128, cols * 8, 128), f32),
        pltpu.VMEM((states // 2, 8, chans), f32),
        pltpu.VMEM((height, 8, chans), f32),
        pltpu.VMEM((height, 8, chans), f32),
        pltpu.VMEM((height, 8, 128), f32),
        pltpu.VMEM((chans // 128, height * 8, 128), f32),
        pltpu.VMEM((chans // 128, height * 8, 128), f32),
        pltpu.VMEM((n, 16, 128), bf16),
        pltpu.VMEM((n, 16, 128), bf16),
        pltpu.SemaphoreType.DMA((2,)),
        pltpu.SemaphoreType.DMA((2,)),
        pltpu.SemaphoreType.DMA((n,)),
        pltpu.SemaphoreType.DMA((n,)),
        pltpu.SemaphoreType.DMA((n,)),
        pltpu.SemaphoreType.DMA((n,)),
    ]
    normed = pl.pallas_call(
        functools.partial(fused_kernel, n),
        out_shape=jax.ShapeDtypeStruct((rows, cols, chans), f32),
        in_specs=[pl.BlockSpec(memory_space=pltpu.VMEM)] * 10,
        out_specs=pl.BlockSpec(memory_space=pltpu.VMEM),
        scratch_shapes=scratch,
        compiler_params=pltpu.CompilerParams(
            collective_id=0, has_side_effects=True, vmem_limit_bytes=40 * 1024 * 1024
        ),
    )(
        x_in.transpose(1, 2, 0),
        conv_weight.T,
        conv_bias[None, :],
        proj_weight,
        dt_weight.transpose(0, 2, 1),
        dt_bias,
        decay_rate.transpose(0, 2, 1),
        skip_gain,
        norm_gain[None, :],
        norm_bias[None, :],
    )
    gate = jax.nn.silu(gate_in.astype(f32))
    return (normed.transpose(2, 0, 1) * gate).astype(bf16)


def on_device(*args):
    n = lax.axis_size("sp")
    chans, rows, cols = args[0].shape
    rank, states = args[5].shape[2], args[7].shape[2]
    fits = (chans, rows, cols, rank, states) == (256, 2, 4 * n, 8, 16)
    if lax.axis_size("ch") == 1 and fits:
        return fused_device(n, *args)
    return plain_device(*args)


def solution(mesh):
    placed = (
        P("ch", "sp", None),
        P("ch", "sp", None),
        P("ch", None),
        P("ch"),
        P(None, None, "ch"),
        P(None, "ch", None),
        P(None, "ch"),
        P(None, "ch", None),
        P(None, "ch"),
        P("ch"),
        P("ch"),
    )
    return jax.shard_map(
        on_device, mesh=mesh, in_specs=placed, out_specs=P("ch", "sp", None), check_vma=False
    )
```

profile of v0, /device:TPU:0, one launch (start us, length us, event | category | flops | bytes accessed | tf_op | source)
XLA Modules:
  0.0 38.0 jit_solution(10640061174523131301)
XLA Ops:
  0.0 0.0 copy-start
  0.0 0.0 copy-start.1
  0.0 0.0 copy-start.2
  0.0 0.0 copy-start.3
  0.0 0.0 copy-start.4
  0.0 0.0 copy-start.5
  0.0 0.0 copy-start.7
  0.0 0.0 copy-start.8
  0.0 1.1 %copy.12 = bf16[256,2,128]{0,2,1:T(8,128)(2,1)S(1)} copy(bf16[256,2,128]{2,1,0:T(2,128)(2,1)} %param.11) | data formatting | bytes 262144 | tf_op args[0]
  1.2 0.0 copy-start.6
  1.2 0.0 copy-done
  1.2 0.0 copy-done.1
  1.2 0.0 copy-done.2
  1.2 0.0 copy-done.3
  1.2 0.0 copy-done.4
  1.2 0.0 copy-done.5
  1.3 0.0 copy-done.7
  1.3 0.0 copy-done.8
  1.3 0.6 %copy-done.6 = f32[256]{0:T(256)S(1)} copy-done((f32[256]{0:T(256)S(1)}, f32[256]{0:T(256)}, u32[]{:S(2)}) %copy-start.6) | copy-done | bytes 1048
  1.9 0.0 copy-start.9
  1.9 35.2 %shard_map.109 = f32[2,128,256]{2,1,0:T(8,128)S(1)} custom-call(bf16[2,128,256]{2,1,0:T(8,128)(2,1)S(1)} %bitcast.11, f32[9,256]{1,0:T(8,128)S(1)} %bitcast.14, f32[1,256]{1,0:T(1,128)S(1)} %bitcast.15, bf16[4,40,256]{2,1,0:T(8,128)(2,1)S(1)} %copy-done, f32[4,8,256]{2,1,0:T(8,128)S(1)} %bitcast.13, f32[4,256]{1,0:T(4,128)S(1)} %copy-done.4, ...), custom_call_target="tpu_custom_call" | custom-call | tf_op jit(solution)/shard_map/pallas_call | solution.py:551
  37.0 0.0 copy-done.9
  37.1 0.1 copy.13
  37.2 0.1 fusion.4
  37.3 0.8 %copy.14 = bf16[256,2,128]{2,1,0:T(2,128)(2,1)} copy(bf16[256,2,128]{0,2,1:T(8,128)(2,1)S(1)} %fusion.4) | data formatting | bytes 262144 | tf_op jit(solution)/shard_map/convert_element_type | solution.py:573
Async XLA Ops:
  0.0 1.2 %copy-start = (bf16[4,40,256]{2,1,0:T(8,128)(2,1)S(1)}, bf16[4,40,256]{2,1,0:T(8,128)(2,1)}, u32[]{:S(2)}) copy-start(bf16[4,40,256]{2,1,0:T(8,128)(2,1)} %pw_ref.1) | copy-start | bytes 245764
  0.0 1.2 %copy-start.1 = (f32[4,256,16]{1,2,0:T(8,128)S(1)}, f32[4,256,16]{1,2,0:T(8,128)}, u32[]{:S(2)}) copy-start(f32[4,256,16]{1,2,0:T(8,128)} %param.18) | copy-start | bytes 196612
  0.0 1.2 %copy-start.2 = (f32[4,256,8]{1,2,0:T(8,128)S(1)}, f32[4,256,8]{1,2,0:T(8,128)}, u32[]{:S(2)}) copy-start(f32[4,256,8]{1,2,0:T(8,128)} %param.16) | copy-start | bytes 98308
  0.0 1.2 %copy-start.3 = (f32[256,9]{0,1:T(8,128)S(1)}, f32[256,9]{0,1:T(8,128)}, u32[]{:S(2)}) copy-start(f32[256,9]{0,1:T(8,128)} %param.13) | copy-start | bytes 27652
  0.0 1.2 %copy-start.4 = (f32[4,256]{1,0:T(4,128)S(1)}, f32[4,256]{1,0:T(4,128)}, u32[]{:S(2)}) copy-start(f32[4,256]{1,0:T(4,128)} %db_ref.1) | copy-start | bytes 12292
  0.0 1.2 %copy-start.5 = (f32[4,256]{1,0:T(4,128)S(1)}, f32[4,256]{1,0:T(4,128)}, u32[]{:S(2)}) copy-start(f32[4,256]{1,0:T(4,128)} %skip_ref.1) | copy-start | bytes 12292
  0.0 1.2 %copy-start.7 = (f32[256]{0:T(256)S(1)}, f32[256]{0:T(256)}, u32[]{:S(2)}) copy-start(f32[256]{0:T(256)} %param.20) | copy-start | bytes 3076
  0.0 1.2 %copy-start.8 = (f32[256]{0:T(256)S(1)}, f32[256]{0:T(256)}, u32[]{:S(2)}) copy-start(f32[256]{0:T(256)} %param.21) | copy-start | bytes 3076
  1.2 0.7 %copy-start.6 = (f32[256]{0:T(256)S(1)}, f32[256]{0:T(256)}, u32[]{:S(2)}) copy-start(f32[256]{0:T(256)} %param.14) | copy-start | bytes 3076
  1.9 35.2 %copy-start.9 = (bf16[256,2,128]{2,1,0:T(2,128)(2,1)S(1)}, bf16[256,2,128]{2,1,0:T(2,128)(2,1)}, u32[]{:S(2)}) copy-start(bf16[256,2,128]{2,1,0:T(2,128)(2,1)} %param.12) | copy-start | bytes 393220
where the time goes:
time: 38.2 us; the launch traced here: 38 us
  Pallas kernels  35.2 us (92%)
  local copies, waits for them, and re-layouts  2.65 us (7%)
    pallas_call x1, Pallas kernels, fused_device(): pl.pallas_call(functools.partial(fused_kernel, n), out_shape=jax.ShapeDty...  35.2 us
    unnamed x22, local copies, waits for them, and re-layouts  1.87 us
    convert_element_type x1, local copies, waits for them, and re-layouts, fused_device(): return (normed.transpose(2, 0, 1) * gate).astype(bf16)  0.78 us

commit v1 on v0

--- a/solution.py
+++ b/solution.py
@@ -9,7 +9,7 @@
 
 SPAN = 64
 MESH = pl.DeviceIdType.MESH
-LOG2E = 1.4426950408889634
+UNROLL = 8
 BEFORE = 64
 
 
@@ -185,6 +185,7 @@
     xv,
     cr,
     wf,
+    wt,
     wd,
     rate_h,
     rate_v,
@@ -295,8 +296,10 @@
         high = full.astype(bf16).astype(f32)
         wd[base : base + rank, :] = high
         wd[base + width : base + width + rank, :] = full - high
+    for first in range(2):
+        wt[first] = wf[256 * first : 256 * first + 256, :].T.astype(bf16)
     for s in range(states):
-        rate_v[s] = -LOG2E * jnp.where(
+        rate_v[s] = -jnp.where(
             dir_v, rate_ref[2, s : s + 1, :], rate_ref[3, s : s + 1, :]
         )
     for s in range(half):
@@ -304,23 +307,23 @@
         upper = jnp.where(
             dir_h, rate_ref[0, s + half : s + half + 1, :], rate_ref[1, s + half : s + half + 1, :]
         )
-        rate_h[s] = -LOG2E * jnp.where(low4, lower, upper)
+        rate_h[s] = -jnp.where(low4, lower, upper)
 
     def prepare(steps, first, dirs, u, dl, p, halves):
-        weights = wf[256 * first : 256 * first + 256, :].astype(bf16)
+        weights = wt[first]
         up = wd[256 * first : 256 * first + 256, :].astype(bf16)
         bias = jnp.where(dirs, db_ref[2 * first : 2 * first + 1], db_ref[2 * first + 1 : 2 * first + 2])
         bias = bias[None]
         pick = dirs[:, 0:128][None]
         lift = low4_one[None]
-        size = 16
+        size = 32
 
         @pl.loop(0, steps // size)
         def _(i):
             at = pl.ds(i * size, size)
             flat = u[at].reshape(size * 8, chans).astype(bf16)
             proj = lax.dot_general(
-                flat, weights, (((1,), (1,)), ((), ())), preferred_element_type=f32
+                flat, weights, (((1,), (0,)), ((), ())), preferred_element_type=f32
             )
             proj = proj.astype(bf16).astype(f32).reshape(size, 8, 256)
             one, two = proj[:, :, 0:128], proj[:, :, 128:256]
@@ -332,7 +335,7 @@
                 both.reshape(size * 8, 256).astype(bf16), up, preferred_element_type=f32
             ).reshape(size, 8, chans)
             pre = pre + bias
-            dl[at] = jnp.maximum(pre, 0.0) + jnp.log1p(jnp.exp(-jnp.abs(pre)))
+            dl[at] = jnp.maximum(pre, 0.0) + jnp.log(1.0 + jnp.exp(-jnp.abs(pre)))
             if halves:
                 own = jnp.where(lift, own, pltpu.roll(own, 128 - half, 2))
             p[at] = own
@@ -343,7 +346,7 @@
         total = None
         new = []
         for s in range(count):
-            decay = jnp.exp2(delta * rate[s])
+            decay = jnp.exp(delta * rate[s])
             b_now = jnp.broadcast_to(tile[:, rank + s : rank + s + 1], (8, chans))
             c_now = jnp.broadcast_to(tile[:, offset + s : offset + s + 1], (8, chans))
             now = decay * state[s] + drive * b_now
@@ -391,7 +394,7 @@
                 t, state, u_h, d_h, p_h, rate_h, ya_h, yb_h, cols - 1, half, rank + states
             )
 
-        return lax.fori_loop(lower, upper, body, state, unroll=2)
+        return lax.fori_loop(lower, upper, body, state, unroll=UNROLL)
 
     state = row_steps(0, BEFORE, tuple(jnp.zeros((8, chans), f32) for _ in range(half)))
     for s in range(half):
@@ -425,10 +428,10 @@
         u_v[t, 0:4, :] = value[0:4]
         u_v[height - 1 - t, 4:8, :] = turned[4:8]
 
-    @pl.loop(0, height // 4)
+    @pl.loop(0, height // 8)
     def _(i):
-        for k in range(4):
-            conv_step(i * 4 + k)
+        for k in range(8):
+            conv_step(i * 8 + k)
 
     prepare(height, 1, dir_v, u_v, d_v, p_v, False)
 
@@ -438,7 +441,7 @@
         )
 
     lax.fori_loop(
-        0, height, col_body, tuple(jnp.zeros((8, chans), f32) for _ in range(states)), unroll=2
+        0, height, col_body, tuple(jnp.zeros((8, chans), f32) for _ in range(states)), unroll=UNROLL
     )
 
     skip_v = skip_ref[2:3, :] + skip_ref[3:4, :]
@@ -454,13 +457,16 @@
         tile = jnp.where(low4, column_row(2 * j), pltpu.roll(column_row(2 * j + 1), 4, 0))
         return jnp.concatenate([tile[:, 0:128], tile[:, 128:256]], axis=0).astype(bf16)
 
+    @pl.loop(0, n // 8)
+    def _(i):
+        for k in range(8):
+            vsend[i * 8 + k] = column_tile(i * 8 + k)
+
     @pl.loop(1, n)
     def _(d):
-        j = lax.rem(me + d, n)
-        vsend[j] = column_tile(j)
         v_copy(d, me).start()
 
-    vrecv[me] = column_tile(me)
+    vrecv[pl.ds(me, 1)] = vsend[pl.ds(me, 1)]
 
     row_steps(BEFORE, cols, tuple(state_h[s] for s in range(half)))
 
@@ -493,10 +499,10 @@
             normed = (combined - mean) * lax.rsqrt(var + 1e-05)
             out_ref[r, at, :] = normed * gain_ref[...] + nbias_ref[...]
 
-    @pl.loop(0, cols // 16)
+    @pl.loop(0, cols // 32)
     def _(i):
-        finish(2 * i)
-        finish(2 * i + 1)
+        for k in range(4):
+            finish(4 * i + k)
 
 
 def fused_device(
@@ -525,6 +531,7 @@
         pltpu.VMEM((height + 2, 8, chans), f32),
         pltpu.VMEM((rows, cols, chans), f32),
         pltpu.VMEM((512, chans), f32),
+        pltpu.VMEM((2, chans, 256), bf16),
         pltpu.VMEM((512, chans), f32),
         pltpu.VMEM((states // 2, 8, chans), f32),
         pltpu.VMEM((states, 8, chans), f32),

time: 38.2 us -> 32.1 us (0.84)
  Pallas kernels: 35.2 us -> 29.1 us
    pallas_call x1, Pallas kernels: 35.2 us -> 29.1 us  [fused_device(): pl.pallas_call(functools.partial(fused_kernel, n), out_shape=jax.ShapeDty...]
where the time goes in v1:
time: 32.1 us; the launch traced here: 31.9 us
  Pallas kernels  29.1 us (91%)
  local copies, waits for them, and re-layouts  2.65 us (8%)
    pallas_call x1, Pallas kernels, fused_device(): pl.pallas_call(functools.partial(fused_kernel, n), out_shape=jax.ShapeDty...  29.1 us
    unnamed x22, local copies, waits for them, and re-layouts  1.87 us
    convert_element_type x1, local copies, waits for them, and re-layouts, fused_device(): return (normed.transpose(2, 0, 1) * gate).astype(bf16)  0.78 us

profile of v1, /device:TPU:0, one launch (start us, length us, event | category | flops | bytes accessed | tf_op | source)
XLA Modules:
  0.0 31.9 jit_solution(14708819722732477)
XLA Ops:
  0.0 0.0 copy-start
  0.0 0.0 copy-start.1
  0.0 0.0 copy-start.2
  0.0 0.0 copy-start.3
  0.0 0.0 copy-start.4
  0.0 0.0 copy-start.5
  0.0 0.0 copy-start.7
  0.0 0.0 copy-start.8
  0.0 1.1 %copy.12 = bf16[256,2,128]{0,2,1:T(8,128)(2,1)S(1)} copy(bf16[256,2,128]{2,1,0:T(2,128)(2,1)} %param.11) | data formatting | bytes 262144 | tf_op args[0]
  1.2 0.0 copy-start.6
  1.2 0.0 copy-done
  1.2 0.0 copy-done.1
  1.2 0.0 copy-done.2
  1.2 0.0 copy-done.3
  1.2 0.0 copy-done.4
  1.2 0.0 copy-done.5
  1.3 0.0 copy-done.7
  1.3 0.0 copy-done.8
  1.3 0.6 %copy-done.6 = f32[256]{0:T(256)S(1)} copy-done((f32[256]{0:T(256)S(1)}, f32[256]{0:T(256)}, u32[]{:S(2)}) %copy-start.6) | copy-done | bytes 1048
  1.9 0.0 copy-start.9
  1.9 29.1 %shard_map.109 = f32[2,128,256]{2,1,0:T(8,128)S(1)} custom-call(bf16[2,128,256]{2,1,0:T(8,128)(2,1)S(1)} %bitcast.11, f32[9,256]{1,0:T(8,128)S(1)} %bitcast.14, f32[1,256]{1,0:T(1,128)S(1)} %bitcast.15, bf16[4,40,256]{2,1,0:T(8,128)(2,1)S(1)} %copy-done, f32[4,8,256]{2,1,0:T(8,128)S(1)} %bitcast.13, f32[4,256]{1,0:T(4,128)S(1)} %copy-done.4, ...), custom_call_target="tpu_custom_call" | custom-call | tf_op jit(solution)/shard_map/pallas_call | solution.py:558
  31.0 0.0 copy-done.9
  31.0 0.1 copy.13
  31.1 0.1 fusion.4
  31.2 0.8 %copy.14 = bf16[256,2,128]{2,1,0:T(2,128)(2,1)} copy(bf16[256,2,128]{0,2,1:T(8,128)(2,1)S(1)} %fusion.4) | data formatting | bytes 262144 | tf_op jit(solution)/shard_map/convert_element_type | solution.py:580
Async XLA Ops:
  0.0 1.2 %copy-start = (bf16[4,40,256]{2,1,0:T(8,128)(2,1)S(1)}, bf16[4,40,256]{2,1,0:T(8,128)(2,1)}, u32[]{:S(2)}) copy-start(bf16[4,40,256]{2,1,0:T(8,128)(2,1)} %pw_ref.1) | copy-start | bytes 245764
  0.0 1.2 %copy-start.1 = (f32[4,256,16]{1,2,0:T(8,128)S(1)}, f32[4,256,16]{1,2,0:T(8,128)}, u32[]{:S(2)}) copy-start(f32[4,256,16]{1,2,0:T(8,128)} %param.18) | copy-start | bytes 196612
  0.0 1.2 %copy-start.2 = (f32[4,256,8]{1,2,0:T(8,128)S(1)}, f32[4,256,8]{1,2,0:T(8,128)}, u32[]{:S(2)}) copy-start(f32[4,256,8]{1,2,0:T(8,128)} %param.16) | copy-start | bytes 98308
  0.0 1.2 %copy-start.3 = (f32[256,9]{0,1:T(8,128)S(1)}, f32[256,9]{0,1:T(8,128)}, u32[]{:S(2)}) copy-start(f32[256,9]{0,1:T(8,128)} %param.13) | copy-start | bytes 27652
  0.0 1.2 %copy-start.4 = (f32[4,256]{1,0:T(4,128)S(1)}, f32[4,256]{1,0:T(4,128)}, u32[]{:S(2)}) copy-start(f32[4,256]{1,0:T(4,128)} %db_ref.1) | copy-start | bytes 12292
  0.0 1.2 %copy-start.5 = (f32[4,256]{1,0:T(4,128)S(1)}, f32[4,256]{1,0:T(4,128)}, u32[]{:S(2)}) copy-start(f32[4,256]{1,0:T(4,128)} %skip_ref.1) | copy-start | bytes 12292
  0.0 1.2 %copy-start.7 = (f32[256]{0:T(256)S(1)}, f32[256]{0:T(256)}, u32[]{:S(2)}) copy-start(f32[256]{0:T(256)} %param.20) | copy-start | bytes 3076
  0.0 1.2 %copy-start.8 = (f32[256]{0:T(256)S(1)}, f32[256]{0:T(256)}, u32[]{:S(2)}) copy-start(f32[256]{0:T(256)} %param.21) | copy-start | bytes 3076
  1.2 0.7 %copy-start.6 = (f32[256]{0:T(256)S(1)}, f32[256]{0:T(256)}, u32[]{:S(2)}) copy-start(f32[256]{0:T(256)} %param.14) | copy-start | bytes 3076
  1.9 29.1 %copy-start.9 = (bf16[256,2,128]{2,1,0:T(2,128)(2,1)S(1)}, bf16[256,2,128]{2,1,0:T(2,128)(2,1)}, u32[]{:S(2)}) copy-start(bf16[256,2,128]{2,1,0:T(2,128)(2,1)} %param.12) | copy-start | bytes 393220

commit v2 on v1

--- a/solution.py
+++ b/solution.py
@@ -178,6 +178,9 @@
     gain_ref,
     nbias_ref,
     out_ref,
+    xs,
+    xt,
+    normed,
     xpad,
     halo,
     xsend,
@@ -209,7 +212,7 @@
     vs_sem,
     vr_sem,
 ):
-    rows, cols, chans = x_ref.shape
+    rows, cols, chans = cr.shape
     height = rows * n
     rank = dw_ref.shape[1]
     states = rate_ref.shape[1]
@@ -227,22 +230,33 @@
             barrier, inc=1, device_id={"sp": lax.rem(me + d, n)}, device_id_type=MESH
         )
 
+    low4_one = lax.broadcasted_iota(jnp.int32, (8, 128), 0) < 4
+    low6 = lax.broadcasted_iota(jnp.int32, (8, chans), 0) < 6
+
     edge = jnp.zeros((rows + 2, 8, chans), f32)
     xpad[:, 0:8, :] = edge
     xpad[:, cols + 8 : cols + 16, :] = edge
+    xs[...] = x_ref[...].astype(f32)
     for r in range(rows):
-        xpad[r + 1, 8 : cols + 8, :] = x_ref[r].astype(f32)
+        upright = xs[pl.ds(r, chans, stride=rows), :].T
+        xpad[r + 1, 8 : cols + 8, :] = upright
+        xt[r] = upright.astype(bf16)
     for j in range(n):
-        at = 8 + 4 * j - 2
-        pair = [xpad[r + 1, at : at + 8, :] for r in range(rows)]
-        xsend[j] = jnp.concatenate(pair, axis=0).astype(bf16)
+        at = 8 + 4 * j - 1
+        first, second = xpad[1, at : at + 8, :], xpad[2, at : at + 8, :]
+        lower = jnp.where(low6, first, pltpu.roll(second, 6, 0))
+        rest = pltpu.roll(second, 6, 0)
+        near, far = rest[:, 0:128], pltpu.roll(rest[:, 128:256], 4, 0)
+        xsend[j] = jnp.concatenate(
+            [lower[:, 0:128], lower[:, 128:256], jnp.where(low4_one, near, far)], axis=0
+        ).astype(bf16)
     xrecv[pl.ds(me, 1)] = xsend[pl.ds(me, 1)]
 
     pl.semaphore_wait(barrier, n - 1)
 
     def halo_copy(which):
         return pltpu.make_async_remote_copy(
-            src_ref=x_ref.at[rows - 1 if which == 0 else 0],
+            src_ref=xt.at[rows - 1 if which == 0 else 0],
             dst_ref=halo.at[which],
             send_sem=halo_send.at[which],
             recv_sem=halo_recv.at[which],
@@ -264,13 +278,12 @@
             device_id_type=MESH,
         )
 
-    def v_copy(d, slot):
-        dst = lax.rem(me + d, n)
+    def v_copy(dst, slot):
         return pltpu.make_async_remote_copy(
             src_ref=vsend.at[dst],
             dst_ref=vrecv.at[slot],
-            send_sem=vs_sem.at[d],
-            recv_sem=vr_sem.at[d],
+            send_sem=vs_sem.at[dst],
+            recv_sem=vr_sem.at[slot],
             device_id={"sp": dst},
             device_id_type=MESH,
         )
@@ -281,10 +294,9 @@
 
     sub = lax.broadcasted_iota(jnp.int32, (8, chans), 0)
     low4 = sub < 4
+    low2 = sub < 2
     dir_h = (sub // 2) % 2 == 0
     dir_v = low4
-    low4_one = lax.broadcasted_iota(jnp.int32, (8, 128), 0) < 4
-
     wf[...] = jnp.zeros(wf.shape, f32)
     wd[...] = jnp.zeros(wd.shape, f32)
     for k in range(4):
@@ -410,9 +422,12 @@
 
     @pl.loop(0, n)
     def _(j):
-        both = xrecv[j].astype(f32)
-        xv[1 + 2 * j] = both[0:8]
-        xv[2 + 2 * j] = both[8:16]
+        tiles = xrecv[j].astype(f32)
+        rest = tiles[16:24]
+        lower = jnp.concatenate([tiles[0:8], tiles[8:16]], axis=1)
+        rest = jnp.concatenate([rest, pltpu.roll(rest, 4, 0)], axis=1)
+        xv[1 + 2 * j] = lower
+        xv[2 + 2 * j] = jnp.where(low2, pltpu.roll(lower, 2, 0), pltpu.roll(rest, 2, 0))
 
     def conv_step(t):
         total = jnp.zeros((8, chans), f32) + cb_ref[...]
@@ -422,7 +437,7 @@
             for i in range(3):
                 term = cw_ref[3 * i + j : 3 * i + j + 1, :] * tiles[i]
                 part = term if part is None else part + term
-            total = total + pltpu.roll(part, 7 - j, 0)
+            total = total + pltpu.roll(part, (8 - j) % 8, 0)
         value = jax.nn.silu(total).astype(bf16).astype(f32)
         turned = pltpu.roll(value, 4, 0)
         u_v[t, 0:4, :] = value[0:4]
@@ -440,8 +455,8 @@
             t, state, u_v, d_v, p_v, rate_v, ya_v, yb_v, height - 1, states, rank + states
         )
 
-    lax.fori_loop(
-        0, height, col_body, tuple(jnp.zeros((8, chans), f32) for _ in range(states)), unroll=UNROLL
+    state = lax.fori_loop(
+        0, height // 2, col_body, tuple(jnp.zeros((8, chans), f32) for _ in range(states)), unroll=UNROLL
     )
 
     skip_v = skip_ref[2:3, :] + skip_ref[3:4, :]
@@ -457,22 +472,29 @@
         tile = jnp.where(low4, column_row(2 * j), pltpu.roll(column_row(2 * j + 1), 4, 0))
         return jnp.concatenate([tile[:, 0:128], tile[:, 128:256]], axis=0).astype(bf16)
 
-    @pl.loop(0, n // 8)
-    def _(i):
+    def col_part(c, state):
         for k in range(8):
-            vsend[i * 8 + k] = column_tile(i * 8 + k)
+            state = col_body(height // 2 + 8 * c + k, state)
+        for k in range(4):
+            for j in (n // 2 - 4 - 4 * c + k, n // 2 + 4 * c + k):
+                vsend[j] = column_tile(j)
+
+                @pl.when(j != me)
+                def _():
+                    v_copy(j, me).start()
+
+        return state
+
+    lax.fori_loop(0, height // 16, col_part, state)
+
+    vrecv[pl.ds(me, 1)] = vsend[pl.ds(me, 1)]
+
+    row_steps(BEFORE, cols, tuple(state_h[s] for s in range(half)))
 
     @pl.loop(1, n)
     def _(d):
-        v_copy(d, me).start()
-
-    vrecv[pl.ds(me, 1)] = vsend[pl.ds(me, 1)]
-
-    row_steps(BEFORE, cols, tuple(state_h[s] for s in range(half)))
-
-    @pl.loop(1, n)
-    def _(d):
-        v_copy(d, lax.rem(me + n - d, n)).wait()
+        other = lax.rem(me + d, n)
+        v_copy(other, other).wait()
 
     skip_h = skip_ref[0:1, :] + skip_ref[1:2, :]
 
@@ -496,13 +518,16 @@
             combined = flat + upright
             mean = jnp.sum(combined, axis=1, keepdims=True) / chans
             var = jnp.sum(combined * combined, axis=1, keepdims=True) / chans - mean * mean
-            normed = (combined - mean) * lax.rsqrt(var + 1e-05)
-            out_ref[r, at, :] = normed * gain_ref[...] + nbias_ref[...]
+            scaled = (combined - mean) * lax.rsqrt(var + 1e-05)
+            normed[r, at, :] = scaled * gain_ref[...] + nbias_ref[...]
 
     @pl.loop(0, cols // 32)
     def _(i):
         for k in range(4):
             finish(4 * i + k)
+
+    for r in range(rows):
+        out_ref[pl.ds(r, chans, stride=rows), :] = normed[r].T
 
 
 def fused_device(
@@ -524,10 +549,13 @@
     height = rows * n
     f32, bf16 = jnp.float32, jnp.bfloat16
     scratch = [
+        pltpu.VMEM((chans * rows, cols), f32),
+        pltpu.VMEM((rows, cols, chans), bf16),
+        pltpu.VMEM((rows, cols, chans), f32),
         pltpu.VMEM((rows + 2, cols + 16, chans), f32),
         pltpu.VMEM((2, cols, chans), bf16),
-        pltpu.VMEM((n, 16, chans), bf16),
-        pltpu.VMEM((n, 16, chans), bf16),
+        pltpu.VMEM((n, 24, 128), bf16),
+        pltpu.VMEM((n, 24, 128), bf16),
         pltpu.VMEM((height + 2, 8, chans), f32),
         pltpu.VMEM((rows, cols, chans), f32),
         pltpu.VMEM((512, chans), f32),
@@ -557,7 +585,7 @@
     ]
     normed = pl.pallas_call(
         functools.partial(fused_kernel, n),
-        out_shape=jax.ShapeDtypeStruct((rows, cols, chans), f32),
+        out_shape=jax.ShapeDtypeStruct((chans * rows, cols), f32),
         in_specs=[pl.BlockSpec(memory_space=pltpu.VMEM)] * 10,
         out_specs=pl.BlockSpec(memory_space=pltpu.VMEM),
         scratch_shapes=scratch,
@@ -565,7 +593,7 @@
             collective_id=0, has_side_effects=True, vmem_limit_bytes=40 * 1024 * 1024
         ),
     )(
-        x_in.transpose(1, 2, 0),
+        x_in.reshape(chans * rows, cols),
         conv_weight.T,
         conv_bias[None, :],
         proj_weight,
@@ -577,7 +605,7 @@
         norm_bias[None, :],
     )
     gate = jax.nn.silu(gate_in.astype(f32))
-    return (normed.transpose(2, 0, 1) * gate).astype(bf16)
+    return (normed.reshape(chans, rows, cols) * gate).astype(bf16)
 
 
 def on_device(*args):

time: 32.1 us -> 35.2 us (1.097)
  local copies, waits for them, and re-layouts: 2.65 us -> 4.84 us
  other arithmetic: 0.08 us -> 0.94 us
    unnamed x22, local copies, waits for them, and re-layouts: 1.87 us -> 4.84 us
    convert_element_type x1, other arithmetic: 0.08 us -> 0.94 us  [fused_device(): return (normed.reshape(chans, rows, cols) * gate).astype(bf16)]
    convert_element_type x1 -> x0, local copies, waits for them, and re-layouts: 0.78 us -> none  [fused_device(): return (normed.transpose(2, 0, 1) * gate).astype(bf16)]
where the time goes in v2:
time: 35.2 us; the launch traced here: 34.9 us
  Pallas kernels  29 us (82%)
  local copies, waits for them, and re-layouts  4.84 us (14%)
  other arithmetic  0.94 us (3%)
    pallas_call x1, Pallas kernels, fused_device(): pl.pallas_call(functools.partial(fused_kernel, n), out_shape=jax.ShapeDty...  29 us
    unnamed x22, local copies, waits for them, and re-layouts  4.84 us
    convert_element_type x1, other arithmetic, fused_device(): return (normed.reshape(chans, rows, cols) * gate).astype(bf16)  0.94 us

profile of v2, /device:TPU:0, one launch (start us, length us, event | category | flops | bytes accessed | tf_op | source)
XLA Modules:
  0.0 34.9 jit_solution(15443867386012175752)
XLA Ops:
  0.0 0.0 copy-start.8
  0.0 0.0 copy-start.9
  0.0 0.0 copy-start.6
  0.0 0.0 copy-start.5
  0.0 0.0 copy-start.7
  0.0 0.7 %copy-done.8 = f32[256]{0:T(256)S(1)} copy-done((f32[256]{0:T(256)S(1)}, f32[256]{0:T(256)}, u32[]{:S(2)}) %copy-start.8) | copy-done | bytes 1048
  0.7 0.0 copy-done.9
  0.7 0.0 copy-done.6
  0.7 0.0 copy-done.5
  0.7 0.0 copy-done.7
  0.7 0.0 copy-start
  0.7 0.9 %copy-done = bf16[256,2,128]{2,1,0:T(2,128)(2,1)S(1)} copy-done((bf16[256,2,128]{2,1,0:T(2,128)(2,1)S(1)}, bf16[256,2,128]{2,1,0:T(2,128)(2,1)}, u32[]{:S(2)}) %copy-start) | copy-done | bytes 131096
  1.6 0.0 copy-start.1
  1.6 0.9 %copy-done.1 = bf16[4,40,256]{2,1,0:T(8,128)(2,1)S(1)} copy-done((bf16[4,40,256]{2,1,0:T(8,128)(2,1)S(1)}, bf16[4,40,256]{2,1,0:T(8,128)(2,1)}, u32[]{:S(2)}) %copy-start.1) | copy-done | bytes 81944
  2.5 0.0 copy-start.2
  2.5 0.8 %copy-done.2 = f32[4,256,16]{1,2,0:T(8,128)S(1)} copy-done((f32[4,256,16]{1,2,0:T(8,128)S(1)}, f32[4,256,16]{1,2,0:T(8,128)}, u32[]{:S(2)}) %copy-start.2) | copy-done | bytes 65560
  3.4 0.0 copy-start.3
  3.4 0.8 %copy-done.3 = f32[4,256,8]{1,2,0:T(8,128)S(1)} copy-done((f32[4,256,8]{1,2,0:T(8,128)S(1)}, f32[4,256,8]{1,2,0:T(8,128)}, u32[]{:S(2)}) %copy-start.3) | copy-done | bytes 32792
  4.1 0.0 copy-start.4
  4.1 0.7 %copy-done.4 = f32[256,9]{0,1:T(8,128)S(1)} copy-done((f32[256,9]{0,1:T(8,128)S(1)}, f32[256,9]{0,1:T(8,128)}, u32[]{:S(2)}) %copy-start.4) | copy-done | bytes 9240
  4.9 0.0 copy-start.10
  4.9 29.0 %shard_map.109 = f32[512,128]{1,0:T(8,128)S(1)} custom-call(bf16[512,128]{1,0:T(8,128)(2,1)S(1)} %bitcast.9, f32[9,256]{1,0:T(8,128)S(1)} %bitcast.12, f32[1,256]{1,0:T(1,128)S(1)} %bitcast.13, bf16[4,40,256]{2,1,0:T(8,128)(2,1)S(1)} %copy-done.1, f32[4,8,256]{2,1,0:T(8,128)S(1)} %bitcast.11, f32[4,256]{1,0:T(4,128)S(1)} %copy-done.5, ...), custom_call_target="tpu_custom_call" | custom-call | tf_op jit(solution)/shard_map/pallas_call | solution.py:586
  33.9 0.0 copy-done.10
  33.9 0.9 %fusion.3 = bf16[256,2,128]{2,1,0:T(2,128)(2,1)} fusion(f32[256,2,128]{2,1,0:T(2,128)S(1)} %bitcast.8, bf16[256,2,128]{2,1,0:T(2,128)(2,1)S(1)} %copy-done.10), kind=kLoop, calls=%fused_computation.5 | loop fusion | flops 458752 | bytes 524288 | tf_op jit(solution)/shard_map/convert_element_type | solution.py:608
Async XLA Ops:
  0.0 0.7 %copy-start.8 = (f32[256]{0:T(256)S(1)}, f32[256]{0:T(256)}, u32[]{:S(2)}) copy-start(f32[256]{0:T(256)} %param.20) | copy-start | bytes 3076
  0.0 0.7 %copy-start.9 = (f32[256]{0:T(256)S(1)}, f32[256]{0:T(256)}, u32[]{:S(2)}) copy-start(f32[256]{0:T(256)} %param.21) | copy-start | bytes 3076
  0.0 0.7 %copy-start.6 = (f32[4,256]{1,0:T(4,128)S(1)}, f32[4,256]{1,0:T(4,128)}, u32[]{:S(2)}) copy-start(f32[4,256]{1,0:T(4,128)} %skip_ref.1) | copy-start | bytes 12292
  0.0 0.7 %copy-start.5 = (f32[4,256]{1,0:T(4,128)S(1)}, f32[4,256]{1,0:T(4,128)}, u32[]{:S(2)}) copy-start(f32[4,256]{1,0:T(4,128)} %db_ref.1) | copy-start | bytes 12292
  0.0 0.7 %copy-start.7 = (f32[256]{0:T(256)S(1)}, f32[256]{0:T(256)}, u32[]{:S(2)}) copy-start(f32[256]{0:T(256)} %param.14) | copy-start | bytes 3076
  0.7 0.9 %copy-start = (bf16[256,2,128]{2,1,0:T(2,128)(2,1)S(1)}, bf16[256,2,128]{2,1,0:T(2,128)(2,1)}, u32[]{:S(2)}) copy-start(bf16[256,2,128]{2,1,0:T(2,128)(2,1)} %param.11) | copy-start | bytes 393220
  1.6 0.9 %copy-start.1 = (bf16[4,40,256]{2,1,0:T(8,128)(2,1)S(1)}, bf16[4,40,256]{2,1,0:T(8,128)(2,1)}, u32[]{:S(2)}) copy-start(bf16[4,40,256]{2,1,0:T(8,128)(2,1)} %pw_ref.1) | copy-start | bytes 245764
  2.5 0.8 %copy-start.2 = (f32[4,256,16]{1,2,0:T(8,128)S(1)}, f32[4,256,16]{1,2,0:T(8,128)}, u32[]{:S(2)}) copy-start(f32[4,256,16]{1,2,0:T(8,128)} %param.18) | copy-start | bytes 196612
  3.4 0.8 %copy-start.3 = (f32[4,256,8]{1,2,0:T(8,128)S(1)}, f32[4,256,8]{1,2,0:T(8,128)}, u32[]{:S(2)}) copy-start(f32[4,256,8]{1,2,0:T(8,128)} %param.16) | copy-start | bytes 98308
  4.1 0.7 %copy-start.4 = (f32[256,9]{0,1:T(8,128)S(1)}, f32[256,9]{0,1:T(8,128)}, u32[]{:S(2)}) copy-start(f32[256,9]{0,1:T(8,128)} %param.13) | copy-start | bytes 27652
  4.9 29.1 %copy-start.10 = (bf16[256,2,128]{2,1,0:T(2,128)(2,1)S(1)}, bf16[256,2,128]{2,1,0:T(2,128)(2,1)}, u32[]{:S(2)}) copy-start(bf16[256,2,128]{2,1,0:T(2,128)(2,1)} %param.12) | copy-start | bytes 393220

commit v3 on v2

--- a/solution.py
+++ b/solution.py
@@ -165,53 +165,56 @@
     return (normed * jax.nn.silu(gate_in.astype(jnp.float32))).astype(jnp.bfloat16)
 
 
-def fused_kernel(
-    n,
-    x_ref,
-    cw_ref,
-    cb_ref,
-    pw_ref,
-    dw_ref,
-    db_ref,
-    rate_ref,
-    skip_ref,
-    gain_ref,
-    nbias_ref,
-    out_ref,
-    xs,
-    xt,
-    normed,
-    xpad,
-    halo,
-    xsend,
-    xrecv,
-    xv,
-    cr,
-    wf,
-    wt,
-    wd,
-    rate_h,
-    rate_v,
-    u_h,
-    d_h,
-    p_h,
-    ya_h,
-    yb_h,
-    state_h,
-    u_v,
-    d_v,
-    p_v,
-    ya_v,
-    yb_v,
-    vsend,
-    vrecv,
-    halo_send,
-    halo_recv,
-    xs_sem,
-    xr_sem,
-    vs_sem,
-    vr_sem,
-):
+def fused_kernel(n, *refs):
+    sources, out_ref, held = refs[:10], refs[10], refs[11:21]
+    (
+        x_ref,
+        cw_ref,
+        cb_ref,
+        pw_ref,
+        dw_ref,
+        db_ref,
+        rate_ref,
+        skip_ref,
+        gain_ref,
+        nbias_ref,
+    ) = held
+    (
+        xs,
+        xt,
+        normed,
+        xpad,
+        halo,
+        xsend,
+        xrecv,
+        xv,
+        cr,
+        wf,
+        wt,
+        wd,
+        rate_h,
+        rate_v,
+        u_h,
+        d_h,
+        p_h,
+        ya_h,
+        yb_h,
+        state_h,
+        u_v,
+        d_v,
+        p_v,
+        ya_v,
+        yb_v,
+        vsend,
+        vrecv,
+        halo_send,
+        halo_recv,
+        xs_sem,
+        xr_sem,
+        vs_sem,
+        vr_sem,
+        in_sem,
+    ) = refs[21:]
     rows, cols, chans = cr.shape
     height = rows * n
     rank = dw_ref.shape[1]
@@ -222,6 +225,13 @@
     me = lax.axis_index("sp")
     right, left = lax.rem(me + 1, n), lax.rem(me + n - 1, n)
 
+    loads = [
+        pltpu.make_async_copy(source, target, in_sem.at[i])
+        for i, (source, target) in enumerate(zip(sources, held))
+    ]
+    for load in loads:
+        load.start()
+
     barrier = pltpu.get_barrier_semaphore()
 
     @pl.loop(1, n)
@@ -236,6 +246,7 @@
     edge = jnp.zeros((rows + 2, 8, chans), f32)
     xpad[:, 0:8, :] = edge
     xpad[:, cols + 8 : cols + 16, :] = edge
+    loads[0].wait()
     xs[...] = x_ref[...].astype(f32)
     for r in range(rows):
         upright = xs[pl.ds(r, chans, stride=rows), :].T
@@ -297,6 +308,8 @@
     low2 = sub < 2
     dir_h = (sub // 2) % 2 == 0
     dir_v = low4
+    for load in loads[1:]:
+        load.wait()
     wf[...] = jnp.zeros(wf.shape, f32)
     wd[...] = jnp.zeros(wd.shape, f32)
     for k in range(4):
@@ -583,16 +596,7 @@
         pltpu.SemaphoreType.DMA((n,)),
         pltpu.SemaphoreType.DMA((n,)),
     ]
-    normed = pl.pallas_call(
-        functools.partial(fused_kernel, n),
-        out_shape=jax.ShapeDtypeStruct((chans * rows, cols), f32),
-        in_specs=[pl.BlockSpec(memory_space=pltpu.VMEM)] * 10,
-        out_specs=pl.BlockSpec(memory_space=pltpu.VMEM),
-        scratch_shapes=scratch,
-        compiler_params=pltpu.CompilerParams(
-            collective_id=0, has_side_effects=True, vmem_limit_bytes=40 * 1024 * 1024
-        ),
-    )(
+    operands = (
         x_in.reshape(chans * rows, cols),
         conv_weight.T,
         conv_bias[None, :],
@@ -604,8 +608,19 @@
         norm_gain[None, :],
         norm_bias[None, :],
     )
-    gate = jax.nn.silu(gate_in.astype(f32))
-    return (normed.reshape(chans, rows, cols) * gate).astype(bf16)
+    held = [pltpu.VMEM(a.shape, a.dtype) for a in operands]
+    normed = pl.pallas_call(
+        functools.partial(fused_kernel, n),
+        out_shape=jax.ShapeDtypeStruct((chans * rows, cols), f32),
+        in_specs=[pl.BlockSpec(memory_space=pltpu.HBM)] * len(operands),
+        out_specs=pl.BlockSpec(memory_space=pltpu.VMEM),
+        scratch_shapes=held + scratch + [pltpu.SemaphoreType.DMA((len(operands),))],
+        compiler_params=pltpu.CompilerParams(
+            collective_id=0, has_side_effects=True, vmem_limit_bytes=64 * 1024 * 1024
+        ),
+    )(*operands)
+    gate = jax.nn.silu(gate_in.reshape(chans * rows, cols).astype(f32))
+    return (normed * gate).astype(bf16).reshape(chans, rows, cols)
 
 
 def on_device(*args):

time: 35.2 us -> 31.8 us (0.903)
  local copies, waits for them, and re-layouts: 4.84 us -> 0 us
  Pallas kernels: 29 us -> 29.9 us
  other arithmetic: 0.94 us -> 1.72 us
    unnamed x22 -> x0, local copies, waits for them, and re-layouts: 4.84 us -> none
    pallas_call x1, Pallas kernels: 29 us -> 29.9 us  [fused_device(): pl.pallas_call(functools.partial(fused_kernel, n), out_shape=jax.ShapeDty...]
    convert_element_type x1, other arithmetic: 0.94 us -> 1.72 us  [fused_device(): return (normed * gate).astype(bf16).reshape(chans, rows, cols)]
where the time goes in v3:
time: 31.8 us; the launch traced here: 31.7 us
  Pallas kernels  29.9 us (94%)
  other arithmetic  1.72 us (5%)
    pallas_call x1, Pallas kernels, fused_device(): pl.pallas_call(functools.partial(fused_kernel, n), out_shape=jax.ShapeDty...  29.9 us
    convert_element_type x1, other arithmetic, fused_device(): return (normed * gate).astype(bf16).reshape(chans, rows, cols)  1.72 us

profile of v3, /device:TPU:0, one launch (start us, length us, event | category | flops | bytes accessed | tf_op | source)
XLA Modules:
  0.0 31.7 jit_solution(16608969379225505980)
XLA Ops:
  0.0 29.9 %shard_map.109 = f32[512,128]{1,0:T(8,128)} custom-call(bf16[512,128]{1,0:T(8,128)(2,1)} %bitcast.10, f32[9,256]{1,0:T(8,128)} %bitcast.14, f32[1,256]{1,0:T(1,128)} %bitcast.15, bf16[4,40,256]{2,1,0:T(8,128)(2,1)} %refs_3_.1, f32[4,8,256]{2,1,0:T(8,128)} %bitcast.13, f32[4,256]{1,0:T(4,128)} %refs_5_.1, f32[4,16,256]{2,1,0:T(8,128)} %bitcast.12, ...), custom_call_target="tpu_custom_call" | custom-call | tf_op jit(solution)/shard_map/pallas_call | solution.py:612
  29.9 1.7 %fusion.4 = bf16[512,128]{1,0:T(8,128)(2,1)} fusion(f32[512,128]{1,0:T(8,128)} %shard_map.109, bf16[512,128]{1,0:T(8,128)(2,1)} %bitcast.11), kind=kLoop, calls=%fused_computation.6 | loop fusion | flops 458752 | bytes 524288 | tf_op jit(solution)/shard_map/convert_element_type | solution.py:623

commit v4 on v3

--- a/solution.py
+++ b/solution.py
@@ -9,7 +9,7 @@
 
 SPAN = 64
 MESH = pl.DeviceIdType.MESH
-UNROLL = 8
+UNROLL = 16
 BEFORE = 64
 
 
@@ -166,7 +166,7 @@
 
 
 def fused_kernel(n, *refs):
-    sources, out_ref, held = refs[:10], refs[10], refs[11:21]
+    sources, out_ref, held = refs[:11], refs[11], refs[12:23]
     (
         x_ref,
         cw_ref,
@@ -178,6 +178,7 @@
         skip_ref,
         gain_ref,
         nbias_ref,
+        gate_ref,
     ) = held
     (
         xs,
@@ -214,7 +215,7 @@
         vs_sem,
         vr_sem,
         in_sem,
-    ) = refs[21:]
+    ) = refs[23:]
     rows, cols, chans = cr.shape
     height = rows * n
     rank = dw_ref.shape[1]
@@ -365,6 +366,9 @@
                 own = jnp.where(lift, own, pltpu.roll(own, 128 - half, 2))
             p[at] = own
 
+    def across(column):
+        return jnp.concatenate([jnp.broadcast_to(column, (8, 128))] * (chans // 128), axis=1)
+
     def step(t, state, u, dl, p, rate, ya, yb, last, count, offset):
         delta, tile = dl[t], p[t]
         drive = delta * u[t]
@@ -372,8 +376,8 @@
         new = []
         for s in range(count):
             decay = jnp.exp(delta * rate[s])
-            b_now = jnp.broadcast_to(tile[:, rank + s : rank + s + 1], (8, chans))
-            c_now = jnp.broadcast_to(tile[:, offset + s : offset + s + 1], (8, chans))
+            b_now = across(tile[:, rank + s : rank + s + 1])
+            c_now = across(tile[:, offset + s : offset + s + 1])
             now = decay * state[s] + drive * b_now
             new.append(now)
             term = c_now * now
@@ -540,7 +544,8 @@
             finish(4 * i + k)
 
     for r in range(rows):
-        out_ref[pl.ds(r, chans, stride=rows), :] = normed[r].T
+        xs[pl.ds(r, chans, stride=rows), :] = normed[r].T
+    out_ref[...] = (xs[...] * jax.nn.silu(gate_ref[...].astype(f32))).astype(bf16)
 
 
 def fused_device(
@@ -607,11 +612,12 @@
         skip_gain,
         norm_gain[None, :],
         norm_bias[None, :],
+        gate_in.reshape(chans * rows, cols),
     )
     held = [pltpu.VMEM(a.shape, a.dtype) for a in operands]
-    normed = pl.pallas_call(
+    mixed = pl.pallas_call(
         functools.partial(fused_kernel, n),
-        out_shape=jax.ShapeDtypeStruct((chans * rows, cols), f32),
+        out_shape=jax.ShapeDtypeStruct((chans * rows, cols), bf16),
         in_specs=[pl.BlockSpec(memory_space=pltpu.HBM)] * len(operands),
         out_specs=pl.BlockSpec(memory_space=pltpu.VMEM),
         scratch_shapes=held + scratch + [pltpu.SemaphoreType.DMA((len(operands),))],
@@ -619,8 +625,7 @@
             collective_id=0, has_side_effects=True, vmem_limit_bytes=64 * 1024 * 1024
         ),
     )(*operands)
-    gate = jax.nn.silu(gate_in.reshape(chans * rows, cols).astype(f32))
-    return (normed * gate).astype(bf16).reshape(chans, rows, cols)
+    return mixed.reshape(chans, rows, cols)
 
 
 def on_device(*args):

time: 31.8 us -> 31.4 us (0.987)
  other arithmetic: 1.72 us -> 0 us
  local copies, waits for them, and re-layouts: 0 us -> 1.65 us
    convert_element_type x1 -> x0, other arithmetic: 1.72 us -> none  [fused_device(): return (normed * gate).astype(bf16).reshape(chans, rows, cols)]
    unnamed x0 -> x1, local copies, waits for them, and re-layouts: none -> 1.65 us
    pallas_call x1, Pallas kernels: 29.9 us -> 29.6 us  [fused_device(): pl.pallas_call(functools.partial(fused_kernel, n), out_shape=jax.ShapeDty...]
where the time goes in v4:
time: 31.4 us; the launch traced here: 31.2 us
  Pallas kernels  29.6 us (94%)
  local copies, waits for them, and re-layouts  1.65 us (5%)
    pallas_call x1, Pallas kernels, fused_device(): pl.pallas_call(functools.partial(fused_kernel, n), out_shape=jax.ShapeDty...  29.6 us
    unnamed x1, local copies, waits for them, and re-layouts  1.65 us

profile of v4, /device:TPU:0, one launch (start us, length us, event | category | flops | bytes accessed | tf_op | source)
XLA Modules:
  0.0 31.2 jit_solution(13471693812606136006)
XLA Ops:
  0.0 29.6 %shard_map.109 = bf16[512,128]{1,0:T(8,128)(2,1)} custom-call(bf16[512,128]{1,0:T(8,128)(2,1)} %bitcast.10, f32[9,256]{1,0:T(8,128)} %bitcast.14, f32[1,256]{1,0:T(1,128)} %bitcast.15, bf16[4,40,256]{2,1,0:T(8,128)(2,1)} %refs_3_.1, f32[4,8,256]{2,1,0:T(8,128)} %bitcast.13, f32[4,256]{1,0:T(4,128)} %refs_5_.1, f32[4,16,256]{2,1,0:T(8,128)} %bitcast.12, ...), custom_call_target="tpu_custom_call" | custom-call | tf_op jit(solution)/shard_map/pallas_call | solution.py:618
  29.6 1.7 %copy.13 = bf16[256,2,128]{2,1,0:T(2,128)(2,1)} copy(bf16[256,2,128]{2,1,0:T(2,128)(2,1)} %bitcast.9) | data formatting | bytes 262144

commit v5 on v4

--- a/solution.py
+++ b/solution.py
@@ -10,7 +10,7 @@
 SPAN = 64
 MESH = pl.DeviceIdType.MESH
 UNROLL = 16
-BEFORE = 64
+BEFORE = 96
 
 
 def with_halo(value, sides, width):

time: 31.4 us -> 32.4 us (1.032)
  Pallas kernels: 29.6 us -> 30.6 us
    pallas_call x1, Pallas kernels: 29.6 us -> 30.6 us  [fused_device(): pl.pallas_call(functools.partial(fused_kernel, n), out_shape=jax.ShapeDty...]
where the time goes in v5:
time: 32.4 us; the launch traced here: 32.3 us
  Pallas kernels  30.6 us (94%)
  local copies, waits for them, and re-layouts  1.65 us (5%)
    pallas_call x1, Pallas kernels, fused_device(): pl.pallas_call(functools.partial(fused_kernel, n), out_shape=jax.ShapeDty...  30.6 us
    unnamed x1, local copies, waits for them, and re-layouts  1.65 us

profile of v5, /device:TPU:0, one launch (start us, length us, event | category | flops | bytes accessed | tf_op | source)
XLA Modules:
  0.0 32.3 jit_solution(13269928090739689734)
XLA Ops:
  0.0 30.6 %shard_map.109 = bf16[512,128]{1,0:T(8,128)(2,1)} custom-call(bf16[512,128]{1,0:T(8,128)(2,1)} %bitcast.10, f32[9,256]{1,0:T(8,128)} %bitcast.14, f32[1,256]{1,0:T(1,128)} %bitcast.15, bf16[4,40,256]{2,1,0:T(8,128)(2,1)} %refs_3_.1, f32[4,8,256]{2,1,0:T(8,128)} %bitcast.13, f32[4,256]{1,0:T(4,128)} %refs_5_.1, f32[4,16,256]{2,1,0:T(8,128)} %bitcast.12, ...), custom_call_target="tpu_custom_call" | custom-call | tf_op jit(solution)/shard_map/pallas_call | solution.py:618
  30.6 1.7 %copy.13 = bf16[256,2,128]{2,1,0:T(2,128)(2,1)} copy(bf16[256,2,128]{2,1,0:T(2,128)(2,1)} %bitcast.9) | data formatting | bytes 262144
